TPU v7x, 32 devices: a whole 2x2x4 slice. The times are simulated.
32 devices in a mesh: seq: 8 (over y, x, core), grp: 4 (over z).
Axes of the slice: x: 2, y: 2, z: 4, core: 2. Of those that a mesh axis runs over, the one named last changes fastest.
Arguments:
- prompt_latent: bfloat16 [4, 8, 256, 576], P('grp', None, 'seq'), may hold values from -6 to 6
- lengths: int32 [4, 8], P('grp'), may hold values from 1 to 256, 1024 in all within a row
- assign: int32 [4, 8], P('grp'), may hold values from 0 to 7, each once within a row
- prefix_latent: bfloat16 [128, 576], P(('seq', 'grp')), may hold values from -6 to 6
- queries: bfloat16 [4, 8, 4, 128, 576], P('grp', 'seq'), may hold values from -16 to 16
- new_latent: bfloat16 [4, 8, 4, 576], P('grp', 'seq'), may hold values from -6 to 6
Outputs:
- attended: bfloat16 [4, 8, 4, 128, 512], P('grp', 'seq')
Inputs may be any that keep to these rules, and one draw needn't show every extreme that they name: `lengths`: the 8 prompts of a group hold 1024 tokens together, and in every group one prompt has exactly 256. `assign`: each row of a group names each of its 8 prompts once.
All inputs are finite; a program needn't handle non-finite values.
Results may differ from a plain program's by a relative error of at most 0.0043.
Values may be sent and summed in bfloat16 or wider, within the bound.
A program may use at most 64 MiB of HBM per device.

v0:
```python
import jax
import jax.numpy as jnp
from jax import lax
from jax.sharding import PartitionSpec as P

LAT = 512


SCALE = 192.0 ** (-0.5)
block_rows = 512


def rotate(rotary, position):
    half_width = rotary.shape[-1] // 2
    frequency = 10000.0 ** (-jnp.arange(half_width).astype(jnp.float32) / half_width)
    angles = position[..., None].astype(jnp.float32) * frequency
    lower_part = rotary[..., :half_width].astype(jnp.float32)
    upper_part = rotary[..., half_width:].astype(jnp.float32)
    cosine = jnp.cos(angles)
    sine = jnp.sin(angles)
    return jnp.concatenate(
        [lower_part * cosine - upper_part * sine, lower_part * sine + upper_part * cosine], -1
    )


def absorb(running, query_rows, key_rows, live_mask):
    run_max, run_sum, run_acc = running
    scores = jnp.dot(query_rows, key_rows.T, preferred_element_type=jnp.float32) * SCALE
    if live_mask is not None:
        scores = jnp.where(live_mask, scores, -jnp.inf)
    new_max = jnp.maximum(run_max, jnp.max(scores, -1))
    factor = jnp.exp(run_max - new_max)
    expo = jnp.exp(scores - new_max[:, None])
    weights = expo.astype(jnp.bfloat16)
    run_acc = run_acc * factor[:, None] + jnp.dot(
        weights, key_rows[:, :LAT], preferred_element_type=jnp.float32
    )
    run_sum = run_sum * factor + jnp.sum(expo, -1)
    return (new_max, run_sum, run_acc)


def blockwise(running, query_rows, key_rows):
    total_rows = key_rows.shape[0]
    for block_start in range(0, total_rows, block_rows):
        block_end = min(block_start + block_rows, total_rows)
        running = absorb(running, query_rows, key_rows[block_start:block_end], None)
    return running


def flush_pending(running, query_rows, pending, filled):
    pending_mask = (jnp.arange(block_rows, dtype=jnp.int32) < filled)[None, :]
    return absorb(running, query_rows, pending, pending_mask)


def make_folder(query_rows):

    def add_prefix(state_now, piece, start):
        running, pending, filled = state_now
        piece_rows = piece.shape[0]
        if piece_rows >= block_rows:
            return (blockwise(running, query_rows, piece), pending, filled)
        overflow = filled + piece_rows > block_rows

        def do_flush(state_in):
            return flush_pending(state_in, query_rows, pending, filled)

        def keep_state(state_in):
            return state_in

        running = lax.cond(overflow, do_flush, keep_state, running)
        filled = jnp.where(overflow, jnp.int32(0), filled)
        pending = lax.dynamic_update_slice_in_dim(pending, piece, filled, 0)
        return (running, pending, filled + piece_rows)

    return add_prefix


def shards(prompt_latent, lengths, assign, prefix_latent, queries, new_latent):
    owner_total = lax.axis_size("seq")
    prefix_len = prefix_latent.shape[0] * owner_total * lax.axis_size("grp")
    owner_order = assign[0]
    outgoing = jnp.take(prompt_latent[0], owner_order, axis=0)
    own_index = lax.axis_index("seq")
    prompt_id = owner_order[own_index]
    own_length = lengths[0][prompt_id]
    step_count = queries.shape[2]
    head_count = queries.shape[3]
    row_count = step_count * head_count
    width_all = prefix_latent.shape[1]
    position = prefix_len + own_length + jnp.arange(step_count, dtype=jnp.int32)
    query_local = queries[0, 0]
    query_rot = rotate(query_local[..., LAT:], position[:, None]).astype(jnp.bfloat16)
    query_rows = jnp.concatenate([query_local[..., :LAT], query_rot], -1).reshape(row_count, -1)
    fresh = new_latent[0, 0]
    fresh_rot = rotate(fresh[:, LAT:], position).astype(jnp.bfloat16)
    fresh_rows = jnp.concatenate([fresh[:, :LAT], fresh_rot], -1)
    row_step = jnp.arange(row_count, dtype=jnp.int32) // head_count
    fresh_mask = jnp.arange(step_count, dtype=jnp.int32)[None, :] <= row_step[:, None]
    running = (
        jnp.full((row_count,), -jnp.inf, jnp.float32),
        jnp.zeros((row_count,), jnp.float32),
        jnp.zeros((row_count, LAT), jnp.float32),
    )
    running = absorb(running, query_rows, fresh_rows, fresh_mask)
    add_prefix = make_folder(query_rows)
    start_state = (running, jnp.zeros((block_rows, width_all), jnp.bfloat16), jnp.int32(0))
    running, pending, filled = add_prefix(
        start_state, lax.all_gather(prefix_latent, ("seq", "grp"), axis=0, tiled=True), jnp.int32(0)
    )
    running = lax.cond(
        filled > 0,
        lambda state_in: flush_pending(state_in, query_rows, pending, filled),
        lambda state_in: state_in,
        running,
    )
    arrived = lax.all_to_all(outgoing, "seq", split_axis=0, concat_axis=1, tiled=True)
    own_cache = arrived[0]
    cache_len = own_cache.shape[0]
    block_len = min(block_rows, cache_len)
    block_total = cache_len // block_len

    def cache_step(block_index, state_now):
        block_start = block_index * block_len
        key_rows = lax.dynamic_slice_in_dim(own_cache, block_start, block_len, 0)
        live_mask = (block_start + jnp.arange(block_len, dtype=jnp.int32))[None, :] < own_length

        def take_block(state_in):
            return absorb(state_in, query_rows, key_rows, live_mask)

        def skip_block(state_in):
            return state_in

        return lax.cond(block_start < own_length, take_block, skip_block, state_now)

    running = lax.fori_loop(0, block_total, cache_step, running)
    run_max, run_sum, run_acc = running
    result = (run_acc / run_sum[:, None]).astype(jnp.bfloat16)
    return result.reshape(1, 1, step_count, head_count, LAT)


def solution(mesh):
    placed = (
        P("grp", None, "seq", None),
        P("grp", None),
        P("grp", None),
        P(("seq", "grp"), None),
        P("grp", "seq", None, None, None),
        P("grp", "seq", None, None),
    )
    return jax.shard_map(
        shards,
        mesh=mesh,
        in_specs=placed,
        out_specs=P("grp", "seq", None, None, None),
        check_vma=False,
    )
```

profile of v0, /device:TPU:0, one launch (start us, length us, event | category | flops | bytes accessed | tf_op | source)
XLA Modules:
  0.0 89.2 jit_solution(4400689543941473357)
XLA Ops:
  0.0 0.0 copy-start
  0.0 0.7 fusion.34
  0.8 0.7 compare_and_fusion
  1.4 0.0 copy-done
  1.4 0.6 gather_fusion
  2.0 0.0 copy-start.4
  2.1 0.8 broadcast_select_fusion
  2.9 5.2 %all-to-all-start = ((bf16[8,32,576]{2,1,0:T(8,128)(2,1)}), bf16[8,32,576]{2,1,0:T(8,128)(2,1)S(1)}, u32[]{:S(2)}, u32[]{:S(2)}) async-start(bf16[8,32,576]{2,1,0:T(8,128)(2,1)} %broadcast_select_fusion), calls=%async_computation | async-start | bytes 655360 | tf_op jit(solution)/shard_map/all_to_all | solution.py:116
  8.1 0.0 copy-done.6
  8.1 0.7 constant_dynamic-slice_fusion.1
  10.9 0.6 constant_dynamic-slice_fusion
  12.8 0.1 fusion.28
  13.0 0.1 fusion.15
  13.1 0.0 copy-start.5
  13.1 0.3 copy.9
  13.4 0.3 copy-done.5
  13.8 70.3 %all-gather = bf16[32,4,576]{2,1,0:T(4,128)(2,1)S(1)} all-gather(bf16[1,4,576]{2,1,0:T(4,128)(2,1)S(1)} %bitcast.30), channel_id=1, replica_groups=mesh['seq'=8,'grp'=4] {'seq','grp'}, dimensions={0}, use_global_device_ids=true | all-gather | bytes 152064 | tf_op jit(solution)/shard_map/all_gather | solution.py:108
  84.1 0.1 reshape.172
  84.2 0.3 fusion.40
  84.5 0.6 fusion.41
  85.1 0.0 copy-done.1
  85.1 0.2 fusion.10
  85.4 0.4 fusion.6
  85.7 0.3 copy-done.2
  86.1 0.5 convolution_add_fusion.1
  86.5 0.0 all-to-all-done
  86.6 1.7 %conditional.1 = ((f32[512]{0:T(512)S(1)}, f32[512,512]{1,0:T(8,128)S(1)})) conditional(s32[]{:T(128)} %convert_element_type.60, (f32[512]{0:T(512)S(1)}, f32[512,512]{1,0:T(8,128)S(1)}) %tuple.24, (s32[]{:T(128)}, s32[1,256]{1,0:T(1,128)S(1)}, bf16[8,32,576]{2,1,0:T(8,128)(2,1)S(1)}, bf16[512,576]{1,0:T(8,128)(2,1)S(1)}, f32[512]{0:T(512)S(1)}, ...), branch_computations={%region_4.5_spmd, %region_5.8_spmd} | conditional | flops 286655744 | bytes 4847132 | solution.py:133
  86.6 0.6 compare_reduce_fusion
  87.2 0.4 fusion.39
  87.6 0.1 fusion.2
  87.8 0.5 convolution_add_fusion
  88.3 0.9 %divide_convert_fusion = bf16[512,512]{1,0:T(8,128)(2,1)} fusion(f32[512,512]{1,0:T(8,128)S(1)} %get-tuple-element.93, f32[512]{0:T(512)S(1)} %get-tuple-element.94), kind=kLoop, calls=%fused_computation.19 | loop fusion | flops 524288 | bytes 1574912 | tf_op jit(solution)/shard_map/convert_element_type | solution.py:137
  (22 shorter events, 0.2 us)
Async XLA Ops:
  0.0 1.4 %copy-start = (bf16[1,8,32,576]{3,2,1,0:T(8,128)(2,1)S(1)}, bf16[1,8,32,576]{3,2,1,0:T(8,128)(2,1)}, u32[]{:S(2)}) copy-start(bf16[1,8,32,576]{3,2,1,0:T(8,128)(2,1)} %param.8) | copy-start | bytes 884740
  0.0 8.1 %copy-start.6 = (s32[1,8]{1,0:T(1,128)S(1)}, s32[1,8]{1,0:T(1,128)}, u32[]{:S(2)}) copy-start(s32[1,8]{1,0:T(1,128)} %param.10) | copy-start | bytes 100
  0.0 10.8 %copy-start.7 = (s32[1,8]{1,0:T(1,128)S(1)}, s32[1,8]{1,0:T(1,128)}, u32[]{:S(2)}) copy-start(s32[1,8]{1,0:T(1,128)} %param.9) | copy-start | bytes 100
  0.0 12.8 %copy-start.3 = (bf16[1,1,4,128,576]{3,4,2,1,0:T(8,128)(2,1)S(1)}, bf16[1,1,4,128,576]{3,4,2,1,0:T(8,128)(2,1)}, u32[]{:S(2)}) copy-start(bf16[1,1,4,128,576]{3,4,2,1,0:T(8,128)(2,1)} %param.12) | copy-start | bytes 1769476
  2.0 10.8 %copy-start.4 = (bf16[1,1,4,576]{3,2,1,0:T(4,128)(2,1)S(1)}, bf16[1,1,4,576]{3,2,1,0:T(4,128)(2,1)}, u32[]{:S(2)}) copy-start(bf16[1,1,4,576]{3,2,1,0:T(4,128)(2,1)} %param.13) | copy-start | bytes 13828
  2.9 83.6 %all-to-all-start = ((bf16[8,32,576]{2,1,0:T(8,128)(2,1)}), bf16[8,32,576]{2,1,0:T(8,128)(2,1)S(1)}, u32[]{:S(2)}, u32[]{:S(2)}) async-start(bf16[8,32,576]{2,1,0:T(8,128)(2,1)} %broadcast_select_fusion), calls=%async_computation | async-start | bytes 655360 | tf_op jit(solution)/shard_map/all_to_all | solution.py:116
  13.1 0.7 copy-start.5
  84.1 1.0 %copy-start.1 = (bf16[128,576]{1,0:T(8,128)(2,1)}, bf16[128,576]{1,0:T(8,128)(2,1)S(1)}, u32[]{:S(2)}) copy-start(bf16[128,576]{1,0:T(8,128)(2,1)S(1)} %reshape.172) | copy-start | bytes 442372
  85.1 0.9 %copy-start.2 = (bf16[128,576]{1,0:T(8,128)(2,1)S(1)}, bf16[128,576]{1,0:T(8,128)(2,1)}, u32[]{:S(2)}) copy-start(bf16[128,576]{1,0:T(8,128)(2,1)} %copy-done.1) | copy-start | bytes 442372
where the time goes:
time: 89.6 us; the launch traced here: 89.2 us
  blocking collectives  70.3 us (78%)
  starting transfers between devices  5.18 us (6%)
  other arithmetic  4.47 us (5%)
  between operations  3.55 us (4%)
  local copies, waits for them, and re-layouts  3.02 us (3%)
  matrix products  2.65 us (3%)
    all_gather x1, blocking collectives, shards(): lax.all_gather(prefix_latent, ('seq', 'grp'), axis=0, tiled=True)  70.3 us
    all_to_all x1, starting transfers between devices, shards(): lax.all_to_all(outgoing, 'seq', split_axis=0, concat_axis=1, tiled=True)  5.18 us
  transfers between devices with their start and end apart: 1, of which 0 were waited for; matrix products, arithmetic and copies ran while one was open for 4% of the time, Pallas kernels for 0%

commit v1 on v0

v1 whole, which is shorter than its diff:
```python
import functools
import math

import jax
import jax.numpy as jnp
from jax import lax
from jax.experimental import pallas as pl
from jax.experimental.pallas import tpu as pltpu
from jax.sharding import PartitionSpec as P

LAT = 512
SCALE = 192.0 ** (-0.5)
LOG2E = math.log2(math.e)
MESH = pl.DeviceIdType.MESH
CHUNK = 256


def half_swap(x):
    half = x.shape[-1] // 2
    return jnp.concatenate([x[:, half:], x[:, :half]], -1)


def kernel(
    n_seq, n_grp, steps, heads,
    lengths_hbm, assign_hbm, prompt_hbm, prefix_hbm, query_hbm, fresh_hbm,
    out_hbm,
    lengths_s, assign_s, prompt_v, outgoing, arrived, piece_v, pieces, shared, query_v, fresh_v, out_v,
    load_sem, out_sem, block_send, block_recv, piece_send, piece_recv, plane_send, plane_recv,
):
    me = lax.axis_index("seq")
    my_grp = lax.axis_index("grp")
    block = prompt_v.shape[1]
    piece = piece_v.shape[0]
    plane = n_seq * piece
    prefix_len = n_grp * plane
    rows = steps * heads
    width = query_v.shape[1]

    barrier = pltpu.get_barrier_semaphore()
    for k in range(1, n_seq):
        pl.semaphore_signal(barrier, inc=1, device_id={"seq": lax.rem(me + k, n_seq)}, device_id_type=MESH)
    for k in range(1, n_grp):
        pl.semaphore_signal(barrier, inc=1, device_id={"grp": lax.rem(my_grp + k, n_grp)}, device_id_type=MESH)

    loads = [
        pltpu.make_async_copy(src, dst, load_sem.at[i])
        for i, (src, dst) in enumerate([
            (prefix_hbm, piece_v),
            (assign_hbm, assign_s),
            (lengths_hbm, lengths_s),
            (prompt_hbm, prompt_v),
            (fresh_hbm, fresh_v),
            (query_hbm, query_v),
        ])
    ]
    for load in loads:
        load.start()
    prefix_load, assign_load, lengths_load, prompt_load, fresh_load, query_load = loads

    prefix_load.wait()
    pl.semaphore_wait(barrier, n_seq - 1 + n_grp - 1)

    def piece_copy(peer, slot):
        return pltpu.make_async_remote_copy(
            src_ref=piece_v, dst_ref=pieces.at[slot], send_sem=piece_send.at[peer], recv_sem=piece_recv.at[slot],
            device_id={"seq": peer}, device_id_type=MESH,
        )

    for k in range(1, n_seq):
        piece_copy(lax.rem(me + k, n_seq), me).start()

    assign_load.wait()
    prompt_load.wait()

    def block_copy(peer, slot):
        return pltpu.make_async_remote_copy(
            src_ref=outgoing.at[peer], dst_ref=arrived.at[pl.ds(pl.multiple_of(slot * block, block), block)],
            send_sem=block_send.at[peer], recv_sem=block_recv.at[slot],
            device_id={"seq": peer}, device_id_type=MESH,
        )

    for k in range(1, n_seq):
        peer = lax.rem(me + k, n_seq)
        outgoing[peer] = prompt_v[assign_s[0, peer]]
        block_copy(peer, me).start()
    own_id = assign_s[0, me]
    arrived[pl.ds(pl.multiple_of(me * block, block), block)] = prompt_v[own_id]

    lengths_load.wait()
    own_length = lengths_s[0, own_id]
    rotary = width - LAT
    half = rotary // 2
    lane = lax.broadcasted_iota(jnp.int32, (8, rotary), 1)
    row = lax.broadcasted_iota(jnp.int32, (8, rotary), 0)
    lane_half = jnp.where(lane >= half, lane - half, lane)
    frequency = jnp.exp(lane_half.astype(jnp.float32) * (-math.log(10000.0) / half))
    angles = (prefix_len + own_length + row).astype(jnp.float32) * frequency
    cosine = jnp.cos(angles)
    sine = jnp.sin(angles)
    sine = jnp.where(lane >= half, sine, -sine)

    fresh_load.wait()
    fresh = fresh_v[...].astype(jnp.float32)
    fresh_rot = fresh[:, LAT:] * cosine[:steps] + half_swap(fresh[:, LAT:]) * sine[:steps]
    fresh_rows = jnp.concatenate([fresh[:, :LAT], fresh_rot], -1)
    fresh_rows = jnp.concatenate([fresh_rows, jnp.zeros((16 - steps, width), jnp.float32)], 0)
    shared[pl.ds(prefix_len, 16)] = fresh_rows.astype(jnp.bfloat16)

    query_load.wait()
    for t in range(steps):
        x = query_v[pl.ds(t * heads, heads), LAT:].astype(jnp.float32)
        turned = x * cosine[t:t + 1] + half_swap(x) * sine[t:t + 1]
        query_v[pl.ds(t * heads, heads), LAT:] = turned.astype(jnp.bfloat16)

    pieces[me] = piece_v[...]
    for k in range(1, n_seq):
        slot = lax.rem(me + k, n_seq)
        piece_copy(slot, slot).wait_recv()
    plane_rows = jnp.concatenate([pieces[i].astype(jnp.float32) for i in range(n_seq)], 0)
    shared[pl.ds(pl.multiple_of(my_grp * plane, plane), plane)] = plane_rows.astype(jnp.bfloat16)

    def plane_copy(peer, slot):
        here = pl.ds(pl.multiple_of(slot * plane, plane), plane)
        return pltpu.make_async_remote_copy(
            src_ref=shared.at[here], dst_ref=shared.at[here], send_sem=plane_send.at[peer], recv_sem=plane_recv.at[slot],
            device_id={"grp": peer}, device_id_type=MESH,
        )

    for k in range(1, n_grp):
        plane_copy(lax.rem(my_grp + k, n_grp), my_grp).start()
    for k in range(1, n_grp):
        slot = lax.rem(my_grp + k, n_grp)
        plane_copy(slot, slot).wait_recv()

    def score(query, keys):
        return lax.dot_general(query, keys, (((1,), (1,)), ((), ())), preferred_element_type=jnp.float32)

    def attend(s, top, keys):
        e = jnp.exp2((s - top) * (SCALE * LOG2E))
        total = jnp.sum(e, -1, keepdims=True)
        return total, jnp.dot(e.astype(jnp.bfloat16), keys, preferred_element_type=jnp.float32)

    starts = range(0, rows, CHUNK)
    state = []
    for start in starts:
        query = query_v[pl.ds(start, CHUNK)]
        s = score(query, shared[...])
        column = lax.broadcasted_iota(jnp.int32, s.shape, 1)
        step = (start + lax.broadcasted_iota(jnp.int32, s.shape, 0)) // heads
        s = jnp.where(column - prefix_len <= step, s, -jnp.inf)
        top = jnp.max(s, -1, keepdims=True)
        total, acc = attend(s, top, shared[:, :LAT])
        state.append((top, total, acc))

    for k in range(1, n_seq):
        slot = lax.rem(me + k, n_seq)
        block_copy(slot, slot).wait_recv()

    stores = []
    for i, start in enumerate(starts):
        top, total, acc = state[i]
        query = query_v[pl.ds(start, CHUNK)]
        s = score(query, arrived[...])
        column = lax.broadcasted_iota(jnp.int32, s.shape, 1)
        s = jnp.where(column < own_length, s, -jnp.inf)
        new_top = jnp.maximum(top, jnp.max(s, -1, keepdims=True))
        factor = jnp.exp2((top - new_top) * (SCALE * LOG2E))
        more, part = attend(s, new_top, arrived[:, :LAT])
        total = total * factor + more
        result = (acc * factor + part) / total
        out_v[pl.ds(start, CHUNK)] = result.astype(jnp.bfloat16)
        here = pl.ds(start, CHUNK)
        store = pltpu.make_async_copy(out_v.at[here], out_hbm.at[here], out_sem.at[i])
        store.start()
        stores.append(store)

    for k in range(1, n_seq):
        peer = lax.rem(me + k, n_seq)
        piece_copy(peer, me).wait_send()
        block_copy(peer, me).wait_send()
    for k in range(1, n_grp):
        plane_copy(lax.rem(my_grp + k, n_grp), my_grp).wait_send()
    for store in stores:
        store.wait()


def shards(prompt_latent, lengths, assign, prefix_latent, queries, new_latent):
    n_seq, n_grp = lax.axis_size("seq"), lax.axis_size("grp")
    prompt = prompt_latent[0]
    prompts, block, width = prompt.shape
    piece = prefix_latent.shape[0]
    steps, heads = queries.shape[2:4]
    rows = steps * heads
    prefix_len = n_seq * n_grp * piece
    bf16 = jnp.bfloat16
    dma = pltpu.SemaphoreType.DMA
    out = pl.pallas_call(
        functools.partial(kernel, n_seq, n_grp, steps, heads),
        out_shape=jax.ShapeDtypeStruct((rows, LAT), bf16),
        in_specs=[pl.BlockSpec(memory_space=pl.ANY)] * 6,
        out_specs=pl.BlockSpec(memory_space=pl.ANY),
        scratch_shapes=[
            pltpu.SMEM(lengths.shape, jnp.int32),
            pltpu.SMEM(assign.shape, jnp.int32),
            pltpu.VMEM(prompt.shape, bf16),
            pltpu.VMEM((n_seq, block, width), bf16),
            pltpu.VMEM((n_seq * block, width), bf16),
            pltpu.VMEM((piece, width), bf16),
            pltpu.VMEM((n_seq, piece, width), bf16),
            pltpu.VMEM((prefix_len + 16, width), bf16),
            pltpu.VMEM((rows, width), bf16),
            pltpu.VMEM((steps, width), bf16),
            pltpu.VMEM((rows, LAT), bf16),
            dma((6,)),
            dma((rows // CHUNK,)),
            dma((n_seq,)), dma((n_seq,)),
            dma((n_seq,)), dma((n_seq,)),
            dma((n_grp,)), dma((n_grp,)),
        ],
        compiler_params=pltpu.CompilerParams(
            collective_id=0, has_side_effects=True, vmem_limit_bytes=48 * 1024 * 1024
        ),
    )(lengths, assign, prompt, prefix_latent, queries.reshape(rows, width), new_latent[0, 0])
    return out.reshape(1, 1, steps, heads, LAT)


def solution(mesh):
    placed = (
        P("grp", None, "seq", None),
        P("grp", None),
        P("grp", None),
        P(("seq", "grp"), None),
        P("grp", "seq", None, None, None),
        P("grp", "seq", None, None),
    )
    return jax.shard_map(
        shards,
        mesh=mesh,
        in_specs=placed,
        out_specs=P("grp", "seq", None, None, None),
        check_vma=False,
    )
```

time: 89.6 us -> 19.8 us (0.22)
  blocking collectives: 70.3 us -> 0 us
  Pallas kernels: 0 us -> 16.8 us
  starting transfers between devices: 5.18 us -> 0 us
  other arithmetic: 4.47 us -> 0 us
  between operations: 3.55 us -> 0.06 us
  matrix products: 2.65 us -> 0 us
    all_gather x1 -> x0, blocking collectives: 70.3 us -> none  [shards(): lax.all_gather(prefix_latent, ('seq', 'grp'), axis=0, tiled=True)]
    pallas_call x0 -> x1, Pallas kernels: none -> 16.8 us  [shards(): pl.pallas_call(functools.partial(kernel, n_seq, n_grp, steps, heads), out...]
    all_to_all x1 -> x0, starting transfers between devices: 5.18 us -> none  [shards(): lax.all_to_all(outgoing, 'seq', split_axis=0, concat_axis=1, tiled=True)]
    dot_general x6 -> x0, matrix products: 2.65 us -> none  [the longest x3 1.33 us: absorb(): jnp.dot(query_rows, key_rows.T, preferred_element_type=jnp.float32) * SCALE]
    unnamed x17 -> x12, local copies, waits for them, and re-layouts: 0.76 us -> 2.84 us
    select_n x3 -> x0, other arithmetic: 1.57 us -> none  [the longest x2 1.57 us: shards(): outgoing = jnp.take(prompt_latent[0], owner_order, axis=0)]
    dynamic_slice x2 -> x0, local copies, waits for them, and re-layouts: 1.3 us -> none  [the longest x1 0.67 us: shards(): prompt_id = owner_order[own_index]]
    convert_element_type x2 -> x0, other arithmetic: 0.94 us -> none  [the longest x1 0.94 us: shards(): result = (run_acc / run_sum[:, None]).astype(jnp.bfloat16)]
  transfers between devices with their start and end apart: 1 -> 0, of which waited for: 0 -> 0; matrix products, arithmetic and copies ran while one was open for 4% -> 0% of each run, Pallas kernels for 0% -> 0%
where the time goes in v1:
time: 19.8 us; the launch traced here: 19.7 us
  Pallas kernels  16.8 us (85%)
  local copies, waits for them, and re-layouts  2.84 us (14%)
    pallas_call x1, Pallas kernels, shards(): pl.pallas_call(functools.partial(kernel, n_seq, n_grp, steps, heads), out...  16.8 us
    unnamed x12, local copies, waits for them, and re-layouts  2.84 us

profile of v1, /device:TPU:0, one launch (start us, length us, event | category | flops | bytes accessed | tf_op | source)
XLA Modules:
  0.0 19.7 jit_solution(10922271977088896811)
XLA Ops:
  0.0 0.0 copy-start
  0.0 0.0 copy-start.1
  0.0 0.0 copy-start.2
  0.0 1.4 %copy.7 = bf16[1,1,4,128,576]{4,3,2,1,0:T(8,128)(2,1)S(1)} copy(bf16[1,1,4,128,576]{3,4,2,1,0:T(8,128)(2,1)} %param.10) | data formatting | bytes 1179648 | tf_op args[4]
  1.4 0.0 copy-start.3
  1.4 0.0 copy-start.4
  1.4 0.0 copy-done
  1.4 0.0 copy-done.1
  1.5 0.0 copy-done.2
  1.5 0.6 %copy-done.3 = s32[1,8]{1,0:T(1,128)S(1)} copy-done((s32[1,8]{1,0:T(1,128)S(1)}, s32[1,8]{1,0:T(1,128)}, u32[]{:S(2)}) %copy-start.3) | copy-done | bytes 56
  2.1 0.0 copy-done.4
  2.1 16.8 %shard_map.64 = bf16[512,512]{1,0:T(8,128)(2,1)S(1)} custom-call(s32[1,8]{1,0:T(1,128)S(1)} %copy-done.3, s32[1,8]{1,0:T(1,128)S(1)} %copy-done.4, bf16[8,32,576]{2,1,0:T(8,128)(2,1)S(1)} %bitcast.6, bf16[4,576]{1,0:T(4,128)(2,1)S(1)} %copy-done.1, bf16[512,576]{1,0:T(8,128)(2,1)S(1)} %bitcast.4, bf16[4,576]{1,0:T(4,128)(2,1)S(1)} %bitcast.7), custom_call_target="tpu_custom_call" | custom-call | tf_op jit(solution)/shard_map/pallas_call | solution.py:197
  18.9 0.8 %copy.9 = bf16[1,1,4,128,512]{4,3,2,1,0:T(8,128)(2,1)} copy(bf16[1,1,4,128,512]{4,3,2,1,0:T(8,128)(2,1)S(1)} %bitcast.5) | data formatting | bytes 1048576
Async XLA Ops:
  0.0 1.4 %copy-start = (bf16[1,8,32,576]{3,2,1,0:T(8,128)(2,1)S(1)}, bf16[1,8,32,576]{3,2,1,0:T(8,128)(2,1)}, u32[]{:S(2)}) copy-start(bf16[1,8,32,576]{3,2,1,0:T(8,128)(2,1)} %param.6) | copy-start | bytes 884740
  0.0 1.4 %copy-start.1 = (bf16[4,576]{1,0:T(4,128)(2,1)S(1)}, bf16[4,576]{1,0:T(4,128)(2,1)}, u32[]{:S(2)}) copy-start(bf16[4,576]{1,0:T(4,128)(2,1)} %prefix_hbm.1) | copy-start | bytes 13828
  0.0 1.5 %copy-start.2 = (bf16[1,1,4,576]{3,2,1,0:T(4,128)(2,1)S(1)}, bf16[1,1,4,576]{3,2,1,0:T(4,128)(2,1)}, u32[]{:S(2)}) copy-start(bf16[1,1,4,576]{3,2,1,0:T(4,128)(2,1)} %param.11) | copy-start | bytes 13828
  1.4 0.7 %copy-start.3 = (s32[1,8]{1,0:T(1,128)S(1)}, s32[1,8]{1,0:T(1,128)}, u32[]{:S(2)}) copy-start(s32[1,8]{1,0:T(1,128)} %lengths_hbm.1) | copy-start | bytes 100
  1.4 0.7 %copy-start.4 = (s32[1,8]{1,0:T(1,128)S(1)}, s32[1,8]{1,0:T(1,128)}, u32[]{:S(2)}) copy-start(s32[1,8]{1,0:T(1,128)} %assign_hbm.1) | copy-start | bytes 100

commit v2 on v1

v2 whole, which is shorter than its diff:
```python
import functools
import math

import jax
import jax.numpy as jnp
from jax import lax
from jax.experimental import pallas as pl
from jax.experimental.pallas import tpu as pltpu
from jax.sharding import PartitionSpec as P

LAT = 512
SCALE = 192.0 ** (-0.5)
LOG2E = math.log2(math.e)
MESH = pl.DeviceIdType.MESH
CHUNK = 256


def half_swap(x):
    half = x.shape[-1] // 2
    return jnp.concatenate([x[:, half:], x[:, :half]], -1)


def kernel(
    n_seq, n_grp,
    lengths_hbm, assign_hbm, prompt_hbm, prefix_hbm, query_hbm, fresh_hbm,
    out_hbm,
    lengths_s, assign_s, prompt_v, outgoing, piece_v, pieces, keys, query_v, fresh_v, out_v,
    load_sem, query_sem, out_sem, block_send, block_recv, piece_send, piece_recv, plane_send, plane_recv,
):
    me = lax.axis_index("seq")
    my_grp = lax.axis_index("grp")
    steps, width, heads = query_hbm.shape
    block = prompt_v.shape[1]
    piece = piece_v.shape[0]
    plane = n_seq * piece
    prefix_len = n_grp * plane
    cache_len = n_seq * block
    rows = steps * heads

    barrier = pltpu.get_barrier_semaphore()
    for k in range(1, n_seq):
        pl.semaphore_signal(barrier, inc=1, device_id={"seq": lax.rem(me + k, n_seq)}, device_id_type=MESH)
    for k in range(1, n_grp):
        pl.semaphore_signal(barrier, inc=1, device_id={"grp": lax.rem(my_grp + k, n_grp)}, device_id_type=MESH)

    loads = [
        pltpu.make_async_copy(src, dst, load_sem.at[i])
        for i, (src, dst) in enumerate([
            (prefix_hbm, piece_v),
            (assign_hbm, assign_s),
            (prompt_hbm, prompt_v),
            (lengths_hbm, lengths_s),
            (fresh_hbm, fresh_v),
        ])
    ]
    query_loads = [
        pltpu.make_async_copy(query_hbm.at[t], query_v.at[:, pl.ds(t * heads, heads)], query_sem.at[t])
        for t in range(steps)
    ]
    for load in loads + query_loads:
        load.start()
    prefix_load, assign_load, prompt_load, lengths_load, fresh_load = loads

    prefix_load.wait()
    pl.semaphore_wait(barrier, n_seq - 1 + n_grp - 1)

    def piece_copy(peer, slot):
        return pltpu.make_async_remote_copy(
            src_ref=piece_v, dst_ref=pieces.at[slot], send_sem=piece_send.at[peer], recv_sem=piece_recv.at[slot],
            device_id={"seq": peer}, device_id_type=MESH,
        )

    for k in range(1, n_seq):
        piece_copy(lax.rem(me + k, n_seq), me).start()

    assign_load.wait()
    prompt_load.wait()

    def block_copy(peer, slot):
        return pltpu.make_async_remote_copy(
            src_ref=outgoing.at[peer], dst_ref=keys.at[pl.ds(pl.multiple_of(slot * block, block), block)],
            send_sem=block_send.at[peer], recv_sem=block_recv.at[slot],
            device_id={"seq": peer}, device_id_type=MESH,
        )

    for k in range(1, n_seq):
        peer = lax.rem(me + k, n_seq)
        outgoing[peer] = prompt_v[assign_s[0, peer]]
        block_copy(peer, me).start()
    own_id = assign_s[0, me]
    keys[pl.ds(pl.multiple_of(me * block, block), block)] = prompt_v[own_id]

    pieces[me] = piece_v[...]
    for k in range(1, n_seq):
        slot = lax.rem(me + k, n_seq)
        piece_copy(slot, slot).wait_recv()
    plane_rows = jnp.concatenate([pieces[i].astype(jnp.float32) for i in range(n_seq)], 0)
    keys[pl.ds(pl.multiple_of(cache_len + my_grp * plane, plane), plane)] = plane_rows.astype(jnp.bfloat16)

    def plane_copy(peer, slot):
        here = pl.ds(pl.multiple_of(cache_len + slot * plane, plane), plane)
        return pltpu.make_async_remote_copy(
            src_ref=keys.at[here], dst_ref=keys.at[here], send_sem=plane_send.at[peer], recv_sem=plane_recv.at[slot],
            device_id={"grp": peer}, device_id_type=MESH,
        )

    for k in range(1, n_grp):
        plane_copy(lax.rem(my_grp + k, n_grp), my_grp).start()

    lengths_load.wait()
    own_length = lengths_s[0, own_id]
    rotary = width - LAT
    half = rotary // 2
    slope = -math.log(10000.0) / half
    lane = lax.broadcasted_iota(jnp.int32, (8, rotary), 1)
    row = lax.broadcasted_iota(jnp.int32, (8, rotary), 0)
    lane_half = jnp.where(lane >= half, lane - half, lane)
    angles = (prefix_len + own_length + row).astype(jnp.float32) * jnp.exp(lane_half.astype(jnp.float32) * slope)
    sine = jnp.sin(angles)
    sine = jnp.where(lane >= half, sine, -sine)[:steps]
    cosine = jnp.cos(angles)[:steps]
    fresh_load.wait()
    fresh = fresh_v[...].astype(jnp.float32)
    fresh_rot = fresh[:, LAT:] * cosine + half_swap(fresh[:, LAT:]) * sine
    fresh_rows = jnp.concatenate([fresh[:, :LAT], fresh_rot], -1)
    fresh_rows = jnp.concatenate([fresh_rows, jnp.zeros((16 - steps, width), jnp.float32)], 0)
    keys[pl.ds(cache_len + prefix_len, 16)] = fresh_rows.astype(jnp.bfloat16)

    lane = lax.broadcasted_iota(jnp.int32, (half, 128), 1)
    row = lax.broadcasted_iota(jnp.int32, (half, 128), 0)
    angles = (prefix_len + own_length + lane).astype(jnp.float32) * jnp.exp(row.astype(jnp.float32) * slope)
    cosine = jnp.cos(angles)
    sine = jnp.sin(angles)
    for t in range(steps):
        query_loads[t].wait()
        here = pl.ds(t * heads, heads)
        a = query_v[LAT:LAT + half, here].astype(jnp.float32)
        b = query_v[LAT + half:, here].astype(jnp.float32)
        c = jnp.broadcast_to(cosine[:, t:t + 1], a.shape)
        s = jnp.broadcast_to(sine[:, t:t + 1], a.shape)
        query_v[LAT:LAT + half, here] = (a * c - b * s).astype(jnp.bfloat16)
        query_v[LAT + half:, here] = (a * s + b * c).astype(jnp.bfloat16)

    for k in range(1, n_grp):
        slot = lax.rem(my_grp + k, n_grp)
        plane_copy(slot, slot).wait_recv()

    def score(first, count, here):
        return jnp.dot(keys[pl.ds(first, count)], query_v[:, here], preferred_element_type=jnp.float32)

    chunks = [pl.ds(start, CHUNK) for start in range(0, rows, CHUNK)]
    shared = []
    for i, here in enumerate(chunks):
        s = score(cache_len, prefix_len + 16, here)
        key = lax.broadcasted_iota(jnp.int32, s.shape, 0) - prefix_len
        step = (i * CHUNK + lax.broadcasted_iota(jnp.int32, s.shape, 1)) // heads
        shared.append(jnp.where(key <= step, s, -jnp.inf))

    for k in range(1, n_seq):
        slot = lax.rem(me + k, n_seq)
        block_copy(slot, slot).wait_recv()

    stores = []
    for i, here in enumerate(chunks):
        s = score(0, cache_len, here)
        s = jnp.where(lax.broadcasted_iota(jnp.int32, s.shape, 0) < own_length, s, -jnp.inf)
        s = jnp.concatenate([s, shared[i]], 0)
        top = jnp.max(s, 0, keepdims=True)
        e = jnp.exp2((s - top) * (SCALE * LOG2E))
        w = (e * (1.0 / jnp.sum(e, 0, keepdims=True))).astype(jnp.bfloat16)
        result = lax.dot_general(w, keys[:, :LAT], (((0,), (0,)), ((), ())), preferred_element_type=jnp.float32)
        out_v[here] = result.astype(jnp.bfloat16)
        store = pltpu.make_async_copy(out_v.at[here], out_hbm.at[here], out_sem.at[i])
        store.start()
        stores.append(store)

    for k in range(1, n_seq):
        peer = lax.rem(me + k, n_seq)
        piece_copy(peer, me).wait_send()
        block_copy(peer, me).wait_send()
    for k in range(1, n_grp):
        plane_copy(lax.rem(my_grp + k, n_grp), my_grp).wait_send()
    for store in stores:
        store.wait()


def shards(prompt_latent, lengths, assign, prefix_latent, queries, new_latent):
    n_seq, n_grp = lax.axis_size("seq"), lax.axis_size("grp")
    prompt = prompt_latent[0]
    prompts, block, width = prompt.shape
    piece = prefix_latent.shape[0]
    steps, heads = queries.shape[2:4]
    rows = steps * heads
    prefix_len = n_seq * n_grp * piece
    bf16 = jnp.bfloat16
    dma = pltpu.SemaphoreType.DMA
    out = pl.pallas_call(
        functools.partial(kernel, n_seq, n_grp),
        out_shape=jax.ShapeDtypeStruct((rows, LAT), bf16),
        in_specs=[pl.BlockSpec(memory_space=pl.ANY)] * 6,
        out_specs=pl.BlockSpec(memory_space=pl.ANY),
        scratch_shapes=[
            pltpu.SMEM(lengths.shape, jnp.int32),
            pltpu.SMEM(assign.shape, jnp.int32),
            pltpu.VMEM(prompt.shape, bf16),
            pltpu.VMEM((n_seq, block, width), bf16),
            pltpu.VMEM((piece, width), bf16),
            pltpu.VMEM((n_seq, piece, width), bf16),
            pltpu.VMEM((n_seq * block + prefix_len + 16, width), bf16),
            pltpu.VMEM((width, rows), bf16),
            pltpu.VMEM((steps, width), bf16),
            pltpu.VMEM((rows, LAT), bf16),
            dma((5,)),
            dma((steps,)),
            dma((rows // CHUNK,)),
            dma((n_seq,)), dma((n_seq,)),
            dma((n_seq,)), dma((n_seq,)),
            dma((n_grp,)), dma((n_grp,)),
        ],
        compiler_params=pltpu.CompilerParams(
            collective_id=0, has_side_effects=True, vmem_limit_bytes=60 * 1024 * 1024
        ),
    )(lengths, assign, prompt, prefix_latent, queries[0, 0].transpose(0, 2, 1), new_latent[0, 0])
    return out.reshape(1, 1, steps, heads, LAT)


def solution(mesh):
    placed = (
        P("grp", None, "seq", None),
        P("grp", None),
        P("grp", None),
        P(("seq", "grp"), None),
        P("grp", "seq", None, None, None),
        P("grp", "seq", None, None),
    )
    return jax.shard_map(
        shards,
        mesh=mesh,
        in_specs=placed,
        out_specs=P("grp", "seq", None, None, None),
        check_vma=False,
    )
```

time: 19.8 us -> 18.3 us (0.924)
  local copies, waits for them, and re-layouts: 2.84 us -> 1.87 us
  Pallas kernels: 16.8 us -> 16.3 us
    unnamed x12 -> x1, local copies, waits for them, and re-layouts: 2.84 us -> 1.87 us
    pallas_call x1, Pallas kernels: 16.8 us -> 16.3 us  [shards(): pl.pallas_call(functools.partial(kernel, n_seq, n_grp), out_shape=jax.Sha...]
where the time goes in v2:
time: 18.3 us; the launch traced here: 18.1 us
  Pallas kernels  16.3 us (89%)
  local copies, waits for them, and re-layouts  1.87 us (10%)
    pallas_call x1, Pallas kernels, shards(): pl.pallas_call(functools.partial(kernel, n_seq, n_grp), out_shape=jax.Sha...  16.3 us
    unnamed x1, local copies, waits for them, and re-layouts  1.87 us

profile of v2, /device:TPU:0, one launch (start us, length us, event | category | flops | bytes accessed | tf_op | source)
XLA Modules:
  0.0 18.1 jit_solution(4244357779672398656)
XLA Ops:
  0.0 16.3 %shard_map.64 = bf16[512,512]{1,0:T(8,128)(2,1)} custom-call(s32[1,8]{1,0:T(1,128)} %lengths_hbm.1, s32[1,8]{1,0:T(1,128)} %assign_hbm.1, bf16[8,32,576]{2,1,0:T(8,128)(2,1)} %bitcast.8, bf16[4,576]{1,0:T(4,128)(2,1)} %prefix_hbm.1, bf16[4,576,128]{2,1,0:T(8,128)(2,1)} %bitcast.7, bf16[4,576]{1,0:T(4,128)(2,1)} %bitcast.9), custom_call_target="tpu_custom_call" | custom-call | tf_op jit(solution)/shard_map/pallas_call | solution.py:197
  16.3 1.9 %copy.8 = bf16[1,1,4,128,512]{4,3,2,1,0:T(8,128)(2,1)} copy(bf16[1,1,4,128,512]{4,3,2,1,0:T(8,128)(2,1)} %bitcast.6) | data formatting | bytes 1048576

commit v3 on v2

--- a/solution.py
+++ b/solution.py
@@ -23,9 +23,9 @@
 def kernel(
     n_seq, n_grp,
     lengths_hbm, assign_hbm, prompt_hbm, prefix_hbm, query_hbm, fresh_hbm,
-    out_hbm,
-    lengths_s, assign_s, prompt_v, outgoing, piece_v, pieces, keys, query_v, fresh_v, out_v,
-    load_sem, query_sem, out_sem, block_send, block_recv, piece_send, piece_recv, plane_send, plane_recv,
+    out_v,
+    lengths_s, assign_s, prompt_v, outgoing, piece_v, pieces, keys, query_v, fresh_v,
+    load_sem, query_sem, block_send, block_recv, piece_send, piece_recv, plane_send, plane_recv,
 ):
     me = lax.axis_index("seq")
     my_grp = lax.axis_index("grp")
@@ -38,11 +38,6 @@
     rows = steps * heads
 
     barrier = pltpu.get_barrier_semaphore()
-    for k in range(1, n_seq):
-        pl.semaphore_signal(barrier, inc=1, device_id={"seq": lax.rem(me + k, n_seq)}, device_id_type=MESH)
-    for k in range(1, n_grp):
-        pl.semaphore_signal(barrier, inc=1, device_id={"grp": lax.rem(my_grp + k, n_grp)}, device_id_type=MESH)
-
     loads = [
         pltpu.make_async_copy(src, dst, load_sem.at[i])
         for i, (src, dst) in enumerate([
@@ -61,6 +56,11 @@
         load.start()
     prefix_load, assign_load, prompt_load, lengths_load, fresh_load = loads
 
+    for k in range(1, n_seq):
+        pl.semaphore_signal(barrier, inc=1, device_id={"seq": lax.rem(me + k, n_seq)}, device_id_type=MESH)
+    for k in range(1, n_grp):
+        pl.semaphore_signal(barrier, inc=1, device_id={"grp": lax.rem(my_grp + k, n_grp)}, device_id_type=MESH)
+
     prefix_load.wait()
     pl.semaphore_wait(barrier, n_seq - 1 + n_grp - 1)
 
@@ -72,6 +72,23 @@
 
     for k in range(1, n_seq):
         piece_copy(lax.rem(me + k, n_seq), me).start()
+
+    pieces[me] = piece_v[...]
+    for k in range(1, n_seq):
+        slot = lax.rem(me + k, n_seq)
+        piece_copy(slot, slot).wait_recv()
+    plane_rows = jnp.concatenate([pieces[i].astype(jnp.float32) for i in range(n_seq)], 0)
+    keys[pl.ds(pl.multiple_of(cache_len + my_grp * plane, plane), plane)] = plane_rows.astype(jnp.bfloat16)
+
+    def plane_copy(peer, slot):
+        here = pl.ds(pl.multiple_of(cache_len + slot * plane, plane), plane)
+        return pltpu.make_async_remote_copy(
+            src_ref=keys.at[here], dst_ref=keys.at[here], send_sem=plane_send.at[peer], recv_sem=plane_recv.at[slot],
+            device_id={"grp": peer}, device_id_type=MESH,
+        )
+
+    for k in range(1, n_grp):
+        plane_copy(lax.rem(my_grp + k, n_grp), my_grp).start()
 
     assign_load.wait()
     prompt_load.wait()
@@ -89,23 +106,6 @@
         block_copy(peer, me).start()
     own_id = assign_s[0, me]
     keys[pl.ds(pl.multiple_of(me * block, block), block)] = prompt_v[own_id]
-
-    pieces[me] = piece_v[...]
-    for k in range(1, n_seq):
-        slot = lax.rem(me + k, n_seq)
-        piece_copy(slot, slot).wait_recv()
-    plane_rows = jnp.concatenate([pieces[i].astype(jnp.float32) for i in range(n_seq)], 0)
-    keys[pl.ds(pl.multiple_of(cache_len + my_grp * plane, plane), plane)] = plane_rows.astype(jnp.bfloat16)
-
-    def plane_copy(peer, slot):
-        here = pl.ds(pl.multiple_of(cache_len + slot * plane, plane), plane)
-        return pltpu.make_async_remote_copy(
-            src_ref=keys.at[here], dst_ref=keys.at[here], send_sem=plane_send.at[peer], recv_sem=plane_recv.at[slot],
-            device_id={"grp": peer}, device_id_type=MESH,
-        )
-
-    for k in range(1, n_grp):
-        plane_copy(lax.rem(my_grp + k, n_grp), my_grp).start()
 
     lengths_load.wait()
     own_length = lengths_s[0, own_id]
@@ -160,19 +160,16 @@
         slot = lax.rem(me + k, n_seq)
         block_copy(slot, slot).wait_recv()
 
-    stores = []
     for i, here in enumerate(chunks):
         s = score(0, cache_len, here)
         s = jnp.where(lax.broadcasted_iota(jnp.int32, s.shape, 0) < own_length, s, -jnp.inf)
         s = jnp.concatenate([s, shared[i]], 0)
         top = jnp.max(s, 0, keepdims=True)
         e = jnp.exp2((s - top) * (SCALE * LOG2E))
-        w = (e * (1.0 / jnp.sum(e, 0, keepdims=True))).astype(jnp.bfloat16)
+        total = jnp.broadcast_to(jnp.sum(e, 0, keepdims=True), (8, CHUNK)).T[:, :1]
+        w = e.astype(jnp.bfloat16)
         result = lax.dot_general(w, keys[:, :LAT], (((0,), (0,)), ((), ())), preferred_element_type=jnp.float32)
-        out_v[here] = result.astype(jnp.bfloat16)
-        store = pltpu.make_async_copy(out_v.at[here], out_hbm.at[here], out_sem.at[i])
-        store.start()
-        stores.append(store)
+        out_v[here] = (result * (1.0 / total)).astype(jnp.bfloat16)
 
     for k in range(1, n_seq):
         peer = lax.rem(me + k, n_seq)
@@ -180,8 +177,6 @@
         block_copy(peer, me).wait_send()
     for k in range(1, n_grp):
         plane_copy(lax.rem(my_grp + k, n_grp), my_grp).wait_send()
-    for store in stores:
-        store.wait()
 
 
 def shards(prompt_latent, lengths, assign, prefix_latent, queries, new_latent):
@@ -196,9 +191,9 @@
     dma = pltpu.SemaphoreType.DMA
     out = pl.pallas_call(
         functools.partial(kernel, n_seq, n_grp),
-        out_shape=jax.ShapeDtypeStruct((rows, LAT), bf16),
-        in_specs=[pl.BlockSpec(memory_space=pl.ANY)] * 6,
-        out_specs=pl.BlockSpec(memory_space=pl.ANY),
+        out_shape=pltpu.VMEM((rows, LAT), bf16),
+        in_specs=[pl.BlockSpec(memory_space=pltpu.HBM)] * 6,
+        out_specs=pl.BlockSpec(memory_space=pltpu.VMEM),
         scratch_shapes=[
             pltpu.SMEM(lengths.shape, jnp.int32),
             pltpu.SMEM(assign.shape, jnp.int32),
@@ -209,16 +204,14 @@
             pltpu.VMEM((n_seq * block + prefix_len + 16, width), bf16),
             pltpu.VMEM((width, rows), bf16),
             pltpu.VMEM((steps, width), bf16),
-            pltpu.VMEM((rows, LAT), bf16),
             dma((5,)),
             dma((steps,)),
-            dma((rows // CHUNK,)),
             dma((n_seq,)), dma((n_seq,)),
             dma((n_seq,)), dma((n_seq,)),
             dma((n_grp,)), dma((n_grp,)),
         ],
         compiler_params=pltpu.CompilerParams(
-            collective_id=0, has_side_effects=True, vmem_limit_bytes=60 * 1024 * 1024
+            collective_id=0, has_side_effects=True, vmem_limit_bytes=62 * 1024 * 1024
         ),
     )(lengths, assign, prompt, prefix_latent, queries[0, 0].transpose(0, 2, 1), new_latent[0, 0])
     return out.reshape(1, 1, steps, heads, LAT)

time: 18.3 us -> 16.3 us (0.89)
  local copies, waits for them, and re-layouts: 1.87 us -> 0.8 us
  Pallas kernels: 16.3 us -> 15.3 us
    unnamed x1, local copies, waits for them, and re-layouts: 1.87 us -> 0.8 us
    pallas_call x1, Pallas kernels: 16.3 us -> 15.3 us  [shards(): pl.pallas_call(functools.partial(kernel, n_seq, n_grp), out_shape=pltpu.V...]
where the time goes in v3:
time: 16.3 us; the launch traced here: 16.2 us
  Pallas kernels  15.3 us (94%)
  local copies, waits for them, and re-layouts  0.8 us (5%)
    pallas_call x1, Pallas kernels, shards(): pl.pallas_call(functools.partial(kernel, n_seq, n_grp), out_shape=pltpu.V...  15.3 us
    unnamed x1, local copies, waits for them, and re-layouts  0.8 us

profile of v3, /device:TPU:0, one launch (start us, length us, event | category | flops | bytes accessed | tf_op | source)
XLA Modules:
  0.0 16.2 jit_solution(2049447981128585268)
XLA Ops:
  0.0 15.3 %shard_map.64 = bf16[512,512]{1,0:T(8,128)(2,1)S(1)} custom-call(s32[1,8]{1,0:T(1,128)} %lengths_hbm.1, s32[1,8]{1,0:T(1,128)} %assign_hbm.1, bf16[8,32,576]{2,1,0:T(8,128)(2,1)} %bitcast.8, bf16[4,576]{1,0:T(4,128)(2,1)} %prefix_hbm.1, bf16[4,576,128]{2,1,0:T(8,128)(2,1)} %bitcast.7, bf16[4,576]{1,0:T(4,128)(2,1)} %bitcast.9), custom_call_target="tpu_custom_call" | custom-call | tf_op jit(solution)/shard_map/pallas_call | solution.py:192
  15.4 0.8 %copy.8 = bf16[1,1,4,128,512]{4,3,2,1,0:T(8,128)(2,1)} copy(bf16[1,1,4,128,512]{4,3,2,1,0:T(8,128)(2,1)S(1)} %bitcast.6) | data formatting | bytes 1048576

commit v4 on v3

--- a/solution.py
+++ b/solution.py
@@ -32,8 +32,8 @@
     steps, width, heads = query_hbm.shape
     block = prompt_v.shape[1]
     piece = piece_v.shape[0]
-    plane = n_seq * piece
-    prefix_len = n_grp * plane
+    plane = n_grp * piece
+    prefix_len = n_seq * plane
     cache_len = n_seq * block
     rows = steps * heads
 
@@ -56,10 +56,10 @@
         load.start()
     prefix_load, assign_load, prompt_load, lengths_load, fresh_load = loads
 
+    for k in range(1, n_grp):
+        pl.semaphore_signal(barrier, inc=1, device_id={"grp": lax.rem(my_grp + k, n_grp)}, device_id_type=MESH)
     for k in range(1, n_seq):
         pl.semaphore_signal(barrier, inc=1, device_id={"seq": lax.rem(me + k, n_seq)}, device_id_type=MESH)
-    for k in range(1, n_grp):
-        pl.semaphore_signal(barrier, inc=1, device_id={"grp": lax.rem(my_grp + k, n_grp)}, device_id_type=MESH)
 
     prefix_load.wait()
     pl.semaphore_wait(barrier, n_seq - 1 + n_grp - 1)
@@ -67,31 +67,18 @@
     def piece_copy(peer, slot):
         return pltpu.make_async_remote_copy(
             src_ref=piece_v, dst_ref=pieces.at[slot], send_sem=piece_send.at[peer], recv_sem=piece_recv.at[slot],
-            device_id={"seq": peer}, device_id_type=MESH,
-        )
-
-    for k in range(1, n_seq):
-        piece_copy(lax.rem(me + k, n_seq), me).start()
-
-    pieces[me] = piece_v[...]
-    for k in range(1, n_seq):
-        slot = lax.rem(me + k, n_seq)
-        piece_copy(slot, slot).wait_recv()
-    plane_rows = jnp.concatenate([pieces[i].astype(jnp.float32) for i in range(n_seq)], 0)
-    keys[pl.ds(pl.multiple_of(cache_len + my_grp * plane, plane), plane)] = plane_rows.astype(jnp.bfloat16)
-
-    def plane_copy(peer, slot):
-        here = pl.ds(pl.multiple_of(cache_len + slot * plane, plane), plane)
-        return pltpu.make_async_remote_copy(
-            src_ref=keys.at[here], dst_ref=keys.at[here], send_sem=plane_send.at[peer], recv_sem=plane_recv.at[slot],
             device_id={"grp": peer}, device_id_type=MESH,
         )
 
     for k in range(1, n_grp):
-        plane_copy(lax.rem(my_grp + k, n_grp), my_grp).start()
+        piece_copy(lax.rem(my_grp + k, n_grp), my_grp).start()
 
     assign_load.wait()
     prompt_load.wait()
+    for peer in range(n_seq):
+        outgoing[peer] = prompt_v[assign_s[0, peer]]
+    own_id = assign_s[0, me]
+    keys[pl.ds(pl.multiple_of(me * block, block), block)] = prompt_v[own_id]
 
     def block_copy(peer, slot):
         return pltpu.make_async_remote_copy(
@@ -102,10 +89,23 @@
 
     for k in range(1, n_seq):
         peer = lax.rem(me + k, n_seq)
-        outgoing[peer] = prompt_v[assign_s[0, peer]]
         block_copy(peer, me).start()
-    own_id = assign_s[0, me]
-    keys[pl.ds(pl.multiple_of(me * block, block), block)] = prompt_v[own_id]
+    pieces[my_grp] = piece_v[...]
+    for k in range(1, n_grp):
+        slot = lax.rem(my_grp + k, n_grp)
+        piece_copy(slot, slot).wait_recv()
+    plane_rows = jnp.concatenate([pieces[i].astype(jnp.float32) for i in range(n_grp)], 0)
+    keys[pl.ds(pl.multiple_of(cache_len + me * plane, plane), plane)] = plane_rows.astype(jnp.bfloat16)
+
+    def plane_copy(peer, slot):
+        here = pl.ds(pl.multiple_of(cache_len + slot * plane, plane), plane)
+        return pltpu.make_async_remote_copy(
+            src_ref=keys.at[here], dst_ref=keys.at[here], send_sem=plane_send.at[peer], recv_sem=plane_recv.at[slot],
+            device_id={"seq": peer}, device_id_type=MESH,
+        )
+
+    for k in range(1, n_seq):
+        plane_copy(lax.rem(me + k, n_seq), me).start()
 
     lengths_load.wait()
     own_length = lengths_s[0, own_id]
@@ -141,8 +141,8 @@
         query_v[LAT:LAT + half, here] = (a * c - b * s).astype(jnp.bfloat16)
         query_v[LAT + half:, here] = (a * s + b * c).astype(jnp.bfloat16)
 
-    for k in range(1, n_grp):
-        slot = lax.rem(my_grp + k, n_grp)
+    for k in range(1, n_seq):
+        slot = lax.rem(me + k, n_seq)
         plane_copy(slot, slot).wait_recv()
 
     def score(first, count, here):
@@ -173,10 +173,10 @@
 
     for k in range(1, n_seq):
         peer = lax.rem(me + k, n_seq)
-        piece_copy(peer, me).wait_send()
+        plane_copy(peer, me).wait_send()
         block_copy(peer, me).wait_send()
     for k in range(1, n_grp):
-        plane_copy(lax.rem(my_grp + k, n_grp), my_grp).wait_send()
+        piece_copy(lax.rem(my_grp + k, n_grp), my_grp).wait_send()
 
 
 def shards(prompt_latent, lengths, assign, prefix_latent, queries, new_latent):
@@ -200,15 +200,15 @@
             pltpu.VMEM(prompt.shape, bf16),
             pltpu.VMEM((n_seq, block, width), bf16),
             pltpu.VMEM((piece, width), bf16),
-            pltpu.VMEM((n_seq, piece, width), bf16),
+            pltpu.VMEM((n_grp, piece, width), bf16),
             pltpu.VMEM((n_seq * block + prefix_len + 16, width), bf16),
             pltpu.VMEM((width, rows), bf16),
             pltpu.VMEM((steps, width), bf16),
             dma((5,)),
             dma((steps,)),
             dma((n_seq,)), dma((n_seq,)),
+            dma((n_grp,)), dma((n_grp,)),
             dma((n_seq,)), dma((n_seq,)),
-            dma((n_grp,)), dma((n_grp,)),
         ],
         compiler_params=pltpu.CompilerParams(
             collective_id=0, has_side_effects=True, vmem_limit_bytes=62 * 1024 * 1024

time: 16.3 us -> 15.2 us (0.933)
  Pallas kernels: 15.3 us -> 14.2 us
    pallas_call x1, Pallas kernels: 15.3 us -> 14.2 us  [shards(): pl.pallas_call(functools.partial(kernel, n_seq, n_grp), out_shape=pltpu.V...]
where the time goes in v4:
time: 15.2 us; the launch traced here: 15.1 us
  Pallas kernels  14.2 us (93%)
  local copies, waits for them, and re-layouts  0.8 us (5%)
    pallas_call x1, Pallas kernels, shards(): pl.pallas_call(functools.partial(kernel, n_seq, n_grp), out_shape=pltpu.V...  14.2 us
    unnamed x1, local copies, waits for them, and re-layouts  0.8 us

profile of v4, /device:TPU:0, one launch (start us, length us, event | category | flops | bytes accessed | tf_op | source)
XLA Modules:
  0.0 15.1 jit_solution(14888669037339001258)
XLA Ops:
  0.0 14.2 %shard_map.64 = bf16[512,512]{1,0:T(8,128)(2,1)S(1)} custom-call(s32[1,8]{1,0:T(1,128)} %lengths_hbm.1, s32[1,8]{1,0:T(1,128)} %assign_hbm.1, bf16[8,32,576]{2,1,0:T(8,128)(2,1)} %bitcast.8, bf16[4,576]{1,0:T(4,128)(2,1)} %prefix_hbm.1, bf16[4,576,128]{2,1,0:T(8,128)(2,1)} %bitcast.7, bf16[4,576]{1,0:T(4,128)(2,1)} %bitcast.9), custom_call_target="tpu_custom_call" | custom-call | tf_op jit(solution)/shard_map/pallas_call | solution.py:192
  14.3 0.8 %copy.8 = bf16[1,1,4,128,512]{4,3,2,1,0:T(8,128)(2,1)} copy(bf16[1,1,4,128,512]{4,3,2,1,0:T(8,128)(2,1)S(1)} %bitcast.6) | data formatting | bytes 1048576
